TPU v7x, 512 devices: a whole 4x8x8 slice. The times are simulated.
512 devices in a mesh: row: 16 (over y, core), col: 32 (over z, x).
Axes of the slice: x: 4, y: 8, z: 8, core: 2. Of those that a mesh axis runs over, the one named last changes fastest.
Arguments:
- amplitudes: float32 [2, 128, 1048576], P(None, 'row', 'col'), may hold values from -6 to 6
- qubit_order: int32 [11], replicated, may hold values from 0 to 10, each once
Outputs:
- correlators: float32 [32, 32768], P('col', 'row')
Inputs may be any that keep to these rules, and one draw needn't show every extreme that they name: `qubit_order`: a permutation of 0 to 10.
All inputs are finite; a program needn't handle non-finite values.
Results may differ from a plain program's by a relative error of at most 0.0003.
Values sent between devices are 32-bit elements; how exact they have to be, the bound alone decides.
A program may use at most 64 MiB of HBM per device.

v0:
```python
import jax
import jax.numpy as jnp
from jax import lax
from jax.sharding import Mesh
from jax.sharding import PartitionSpec as P

MEASURED_QUBITS = 20
ROW = ("row_0", "row_1")
COL = ("col_0", "col_1")


def copy_for_each(x, axis):
    peers = lax.axis_size(axis)
    return lax.all_to_all(jnp.broadcast_to(x[None], (peers, *x.shape)), axis, 0, 0, tiled=True)


def over_copies(x, axis):
    return copy_for_each(x, axis).sum(axis=0)


def one_axis_at_a_time(x, axes):
    far, near = axes
    return over_copies(over_copies(x, near), far)


def split_up(x, dim, peers):
    dims = x.shape
    pieces = x.reshape(*dims[:dim], peers, dims[dim] // peers, *dims[dim + 1 :])
    return jnp.moveaxis(pieces, dim, 0)


def sent_and_summed(x, axis, dim):
    peers = lax.axis_size(axis)
    pieces = lax.all_to_all(split_up(x, dim, peers), axis, 0, 0, tiled=True)
    return jnp.sum(pieces, axis=0)


def filled_up(lines, peers):
    spare = -lines.shape[0] % peers
    if not spare:
        return lines
    return jnp.concatenate([lines, jnp.zeros((spare, *lines.shape[1:]), lines.dtype)])


def laid_out(pieces, dim):
    dims = list(pieces.shape[1:])
    dims[dim] *= pieces.shape[0]
    return jnp.moveaxis(pieces, 0, dim).reshape(dims)


def collect(x, axis, dim):
    return laid_out(copy_for_each(x, axis), dim)


def nested_sum(x, axes):
    lines = x.reshape(-1)
    own = sent_and_summed(filled_up(lines, lax.axis_size(axes)), axes, 0)
    whole = collect(own, axes, 0)
    return whole[: len(lines)].reshape(x.shape)


def source_index(qubit_order):
    count = qubit_order.shape[0]
    target = jnp.arange(2**count, dtype=jnp.int32)
    source = jnp.zeros_like(target)
    for bit_location in range(count):
        bit_value = jnp.bitwise_and(jnp.right_shift(target, bit_location), 1)
        source = source + jnp.left_shift(bit_value, qubit_order[bit_location])
    return source


def reorder_bits(values, qubit_order):
    perm_span = 2 ** qubit_order.shape[0]
    return jnp.take(values.reshape(-1, perm_span), source_index(qubit_order), axis=1).reshape(-1)


def hadamard_matrix(count):
    extent = 2**count
    row_ids = jnp.arange(extent, dtype=jnp.int32)[:, None]
    col_ids = jnp.arange(extent, dtype=jnp.int32)[None, :]
    common = jnp.bitwise_and(row_ids, col_ids)
    parity = jnp.zeros((extent, extent), jnp.int32)
    for bit_location in range(count):
        parity = parity + jnp.bitwise_and(jnp.right_shift(common, bit_location), 1)
    return (1 - 2 * jnp.bitwise_and(parity, 1)).astype(jnp.float32)


def transform_last(values):
    height, length = values.shape
    total_bits = length.bit_length() - 1
    offset = 0
    while offset < total_bits:
        group_bits = min(7, total_bits - offset)
        group_size = 2**group_bits
        matrix = hadamard_matrix(group_bits)
        blocks = values.reshape(height, length // (group_size * 2**offset), group_size, 2**offset)
        blocks = jnp.einsum("ij,rajb->raib", matrix, blocks, precision=lax.Precision.HIGHEST)
        values = blocks.reshape(height, length)
        offset = offset + group_bits
    return values


def local(amplitudes, qubit_order):
    partial_value = jnp.sum(amplitudes * amplitudes, axis=(0, 1))
    probability_total = one_axis_at_a_time(
        jnp.sum(partial_value), ("row_0", ("row_1", "col_0", "col_1"))
    )
    row_count = lax.axis_size(ROW)
    col_count = lax.axis_size(COL)
    share = partial_value.shape[0] // row_count
    summed = nested_sum(partial_value, ROW)
    walsh_coefficients = transform_last(summed.reshape(1, -1)).reshape(-1)
    locally_held = lax.dynamic_slice_in_dim(walsh_coefficients, lax.axis_index(ROW) * share, share)
    locally_held = reorder_bits(locally_held, qubit_order)
    shard_arrangement = locally_held.reshape(-1, col_count)
    shard_arrangement = lax.all_to_all(
        shard_arrangement, COL, split_axis=1, concat_axis=1, tiled=True
    )
    shard_arrangement = transform_last(shard_arrangement)
    shard_arrangement = lax.all_to_all(
        shard_arrangement, COL, split_axis=1, concat_axis=1, tiled=True
    )
    locally_held = shard_arrangement.reshape(-1)
    normalized_result = locally_held * 2.0 ** (MEASURED_QUBITS / 2) / probability_total
    return normalized_result.reshape(1, -1)


def solution(mesh):
    split = Mesh(mesh.devices.reshape(8, 2, 8, 4), ("row_0", "row_1", "col_0", "col_1"))
    return jax.shard_map(
        local,
        mesh=split,
        in_specs=(P(None, ROW, COL), P()),
        out_specs=P(COL, ROW),
        check_vma=False,
    )
```

profile of v0, /device:TPU:2, one launch (start us, length us, event | category | flops | bytes accessed | tf_op | source)
XLA Modules:
  0.0 115.4 jit_solution(1865666028167512534)
XLA Ops:
  0.0 0.0 copy-start
  0.0 3.3 %multiply_reduce_fusion = (f32[]{:T(128)}, f32[32768]{0:T(1024)}) fusion(f32[2,8,32768]{2,1,0:T(8,128)} %param.2), kind=kLoop, calls=%fused_computation.1 | loop fusion | flops 1540095 | bytes 2228228 | tf_op jit(solution)/shard_map/reduce_sum | solution.py:106
  3.3 7.2 %all-to-all-start = ((f32[16,1,2048]{2,1,0:T(1,128)}), f32[16,1,2048]{2,1,0:T(1,128)S(1)}, u32[]{:S(2)}, u32[]{:S(2)}) async-start(f32[16,1,2048]{2,1,0:T(1,128)} %bitcast.11), calls=%async_computation | async-start | bytes 262144 | tf_op jit(solution)/shard_map/all_to_all | solution.py:34
  10.5 0.0 copy-done
  10.5 0.7 fusion.68
  11.2 8.0 %all-to-all-done = f32[16,1,2048]{2,1,0:T(1,128)S(1)} async-done(((f32[16,1,2048]{2,1,0:T(1,128)}), f32[16,1,2048]{2,1,0:T(1,128)S(1)}, u32[]{:S(2)}, u32[]{:S(2)}) %all-to-all-start) | async-done | bytes 131104 | tf_op jit(solution)/shard_map/all_to_all | solution.py:34
  19.2 0.1 reduce_sum.46
  19.3 0.7 broadcast_in_dim.11
  20.0 3.5 %all-to-all-start.1 = ((f32[16,1,2048]{2,1,0:T(1,128)}), f32[16,1,2048]{2,1,0:T(1,128)S(1)}, u32[]{:S(2)}, u32[]{:S(2)}) async-start(f32[16,1,2048]{2,1,0:T(1,128)} %broadcast_in_dim.11), calls=%async_computation.1 | async-start | bytes 262144 | tf_op jit(solution)/shard_map/all_to_all | solution.py:14
  23.6 7.0 %compare_select_fusion = s32[2048,1]{0,1:T(1,128)S(1)} fusion(s32[]{:T(128)} %bitcast.10, s32[]{:T(128)} %bitcast.9, s32[]{:T(128)} %bitcast.8, s32[]{:T(128)} %bitcast.7, s32[]{:T(128)} %bitcast.6, s32[]{:T(128)} %bitcast.5, s32[]{:T(128)} %bitcast.4, s32[]{:T(128)} %bitcast.3, s32[]{:T(128)} %bitcast.2, s32[]{:T(128)} %bitcast.1, s32[]{:T(128)} %bitcast), kind=kLoop, calls=%fused_computation.13 | loop fusion | flops 94208 | bytes 8236 | tf_op jit(solution)/shard_map/jit(_take)/jit(_where)/select_n | solution.py:74
  30.5 1.7 %all-to-all-done.1 = f32[16,1,2048]{2,1,0:T(1,128)S(1)} async-done(((f32[16,1,2048]{2,1,0:T(1,128)}), f32[16,1,2048]{2,1,0:T(1,128)S(1)}, u32[]{:S(2)}, u32[]{:S(2)}) %all-to-all-start.1) | async-done | bytes 131104 | tf_op jit(solution)/shard_map/all_to_all | solution.py:14
  32.2 1.3 %broadcast_in_dim.13 = f32[64,1,1]{2,1,0:T(1,128)} broadcast(f32[]{:T(128)} %get-tuple-element.5), dimensions={} | broadcast | bytes 260 | tf_op jit(solution)/shard_map/broadcast_in_dim | solution.py:14
  33.5 14.0 %all-to-all-start.4 = ((f32[64,1,1]{2,1,0:T(1,128)}), f32[64,1,1]{2,1,0:T(1,128)S(1)}, u32[]{:S(2)}, u32[]{:S(2)}) async-start(f32[64,1,1]{2,1,0:T(1,128)} %broadcast_in_dim.13), calls=%async_computation.4 | async-start | bytes 65536 | tf_op jit(solution)/shard_map/all_to_all | solution.py:14
  47.5 0.3 fusion.3
  47.8 0.3 convolution_bitcast_fusion
  48.1 0.1 copy.31
  48.2 0.6 convolution_bitcast_fusion.1
  48.9 11.8 %gather_fusion = f32[2048]{0:T(1024)S(1)} fusion(f32[2048]{0:T(1024)S(1)} %dynamic_slice.3, s32[2048]{0:T(1024)S(1)} %broadcast_clamp_fusion), kind=kCustom, calls=%fused_computation | custom fusion | bytes 24576 | tf_op jit(solution)/shard_map/jit(_take)/gather | solution.py:74
  60.7 0.1 gather.7
  60.8 0.1 copy.32
  60.8 7.5 %and_select_fusion = f32[64,32,1]{0,1,2:T(8,128)} fusion(f32[64,32,1]{0,1,2:T(8,128)S(1)} %copy.32, s32[]{:T(128)} %bitcast.10, s32[]{:T(128)} %bitcast.9, s32[]{:T(128)} %bitcast.8, s32[]{:T(128)} %bitcast.7, s32[]{:T(128)} %bitcast.6, s32[]{:T(128)} %bitcast.5, s32[]{:T(128)} %bitcast.4, s32[]{:T(128)} %bitcast.3, s32[]{:T(128)} %bitcast.2, s32[]{:T(128)} %bitcast.1, ...), kind=kLoop, calls=%fused_computation.38 | loop fusion | flops 106496 | bytes 16428 | tf_op jit(solution)/shard_map/jit(_take)/select_n | solution.py:74
  68.3 0.0 all-to-all-done.4
  68.3 9.8 %all-to-all-start.2 = ((f32[64,32,1]{0,2,1:T(1,128)}), f32[64,32,1]{0,2,1:T(1,128)S(1)}, u32[]{:S(2)}, u32[]{:S(2)}) async-start(f32[64,32,1]{0,2,1:T(1,128)} %bitcast.19), calls=%async_computation.2 | async-start | bytes 32768 | tf_op jit(solution)/shard_map/all_to_all | solution.py:116
  78.1 0.7 reduce_sum.48
  78.8 7.9 %all-to-all-done.2 = f32[64,32,1]{0,2,1:T(1,128)S(1)} async-done(((f32[64,32,1]{0,2,1:T(1,128)}), f32[64,32,1]{0,2,1:T(1,128)S(1)}, u32[]{:S(2)}, u32[]{:S(2)}) %all-to-all-start.2) | async-done | bytes 8224 | tf_op jit(solution)/shard_map/all_to_all | solution.py:116
  86.7 1.2 broadcast_in_dim.14
  87.8 5.2 %all-to-all-start.5 = ((f32[8,1,1]{2,1,0:T(1,128)}), f32[8,1,1]{2,1,0:T(1,128)S(1)}, u32[]{:S(2)}, u32[]{:S(2)}) async-start(f32[8,1,1]{2,1,0:T(1,128)} %broadcast_in_dim.14), calls=%async_computation.5 | async-start | bytes 8192 | tf_op jit(solution)/shard_map/all_to_all | solution.py:14
  93.0 0.8 fusion.7
  93.8 6.8 %all-to-all-done.5 = f32[8,1,1]{2,1,0:T(1,128)S(1)} async-done(((f32[8,1,1]{2,1,0:T(1,128)}), f32[8,1,1]{2,1,0:T(1,128)S(1)}, u32[]{:S(2)}, u32[]{:S(2)}) %all-to-all-start.5) | async-done | bytes 64 | tf_op jit(solution)/shard_map/all_to_all | solution.py:14
  100.6 4.7 %all-to-all-start.3 = ((f32[64,32,1]{0,2,1:T(1,128)}), f32[64,32,1]{0,2,1:T(1,128)S(1)}, u32[]{:S(2)}, u32[]{:S(2)}) async-start(f32[64,32,1]{0,2,1:T(1,128)} %bitcast.22), calls=%async_computation.3 | async-start | bytes 32768 | tf_op jit(solution)/shard_map/all_to_all | solution.py:120
  105.4 0.6 reduce_sum.49
  106.0 8.0 %all-to-all-done.3 = f32[64,32,1]{0,2,1:T(1,128)S(1)} async-done(((f32[64,32,1]{0,2,1:T(1,128)}), f32[64,32,1]{0,2,1:T(1,128)S(1)}, u32[]{:S(2)}, u32[]{:S(2)}) %all-to-all-start.3) | async-done | bytes 8224 | tf_op jit(solution)/shard_map/all_to_all | solution.py:120
  114.0 0.6 multiply_divide_fusion
  114.7 0.1 copy.38
  114.7 0.7 div.18
  (3 shorter events, 0.0 us)
Async XLA Ops:
  0.0 10.5 %copy-start = (s32[11]{0:T(128)S(1)}, s32[11]{0:T(128)}, u32[]{:S(2)}) copy-start(s32[11]{0:T(128)} %param.3) | copy-start | bytes 136
  3.3 16.0 %all-to-all-start = ((f32[16,1,2048]{2,1,0:T(1,128)}), f32[16,1,2048]{2,1,0:T(1,128)S(1)}, u32[]{:S(2)}, u32[]{:S(2)}) async-start(f32[16,1,2048]{2,1,0:T(1,128)} %bitcast.11), calls=%async_computation | async-start | bytes 262144 | tf_op jit(solution)/shard_map/all_to_all | solution.py:34
  20.0 12.2 %all-to-all-start.1 = ((f32[16,1,2048]{2,1,0:T(1,128)}), f32[16,1,2048]{2,1,0:T(1,128)S(1)}, u32[]{:S(2)}, u32[]{:S(2)}) async-start(f32[16,1,2048]{2,1,0:T(1,128)} %broadcast_in_dim.11), calls=%async_computation.1 | async-start | bytes 262144 | tf_op jit(solution)/shard_map/all_to_all | solution.py:14
  33.5 34.8 %all-to-all-start.4 = ((f32[64,1,1]{2,1,0:T(1,128)}), f32[64,1,1]{2,1,0:T(1,128)S(1)}, u32[]{:S(2)}, u32[]{:S(2)}) async-start(f32[64,1,1]{2,1,0:T(1,128)} %broadcast_in_dim.13), calls=%async_computation.4 | async-start | bytes 65536 | tf_op jit(solution)/shard_map/all_to_all | solution.py:14
  68.3 18.3 %all-to-all-start.2 = ((f32[64,32,1]{0,2,1:T(1,128)}), f32[64,32,1]{0,2,1:T(1,128)S(1)}, u32[]{:S(2)}, u32[]{:S(2)}) async-start(f32[64,32,1]{0,2,1:T(1,128)} %bitcast.19), calls=%async_computation.2 | async-start | bytes 32768 | tf_op jit(solution)/shard_map/all_to_all | solution.py:116
  87.8 12.8 %all-to-all-start.5 = ((f32[8,1,1]{2,1,0:T(1,128)}), f32[8,1,1]{2,1,0:T(1,128)S(1)}, u32[]{:S(2)}, u32[]{:S(2)}) async-start(f32[8,1,1]{2,1,0:T(1,128)} %broadcast_in_dim.14), calls=%async_computation.5 | async-start | bytes 8192 | tf_op jit(solution)/shard_map/all_to_all | solution.py:14
  100.6 13.4 %all-to-all-start.3 = ((f32[64,32,1]{0,2,1:T(1,128)}), f32[64,32,1]{0,2,1:T(1,128)S(1)}, u32[]{:S(2)}, u32[]{:S(2)}) async-start(f32[64,32,1]{0,2,1:T(1,128)} %bitcast.22), calls=%async_computation.3 | async-start | bytes 32768 | tf_op jit(solution)/shard_map/all_to_all | solution.py:120
where the time goes:
time: 116 us; the launch traced here: 115 us
  starting transfers between devices  44.4 us (38%)
  waiting for transfers between devices  32.5 us (28%)
  other arithmetic  19.8 us (17%)
  local copies, waits for them, and re-layouts  16.7 us (14%)
  matrix products  1.97 us (2%)
    all_to_all x3, starting transfers between devices, copy_for_each(): lax.all_to_all(jnp.broadcast_to(x[None], (peers, *x.shape)), axis, 0, 0,...  22.7 us
    all_to_all x2, waiting for transfers between devices, local(): lax.all_to_all(shard_arrangement, COL, split_axis=1, concat_axis=1, tiled...  15.9 us
    all_to_all x2, starting transfers between devices, local(): lax.all_to_all(shard_arrangement, COL, split_axis=1, concat_axis=1, tiled...  14.5 us
    select_n x2, other arithmetic, reorder_bits(): jnp.take(values.reshape(-1, perm_span), source_index(qubit_order), axis=1)  14.5 us
    gather x3, local copies, waits for them, and re-layouts, reorder_bits(): jnp.take(values.reshape(-1, perm_span), source_index(qubit_order), axis=1)  11.9 us
    all_to_all x3, waiting for transfers between devices, copy_for_each(): lax.all_to_all(jnp.broadcast_to(x[None], (peers, *x.shape)), axis, 0, 0,...  8.53 us
    all_to_all x1, waiting for transfers between devices, sent_and_summed(): pieces = lax.all_to_all(split_up(x, dim, peers), axis, 0, 0, tiled=True)  8.03 us
    all_to_all x1, starting transfers between devices, sent_and_summed(): pieces = lax.all_to_all(split_up(x, dim, peers), axis, 0, 0, tiled=True)  7.21 us
  transfers between devices with their start and end apart: 6, of which 5 were waited for; matrix products, arithmetic and copies ran while one was open for 26% of the time, Pallas kernels for 0%

commit v1 on v0

v1 whole, which is shorter than its diff:
```python
import functools
import itertools

import jax
import jax.numpy as jnp
from jax import lax
from jax.experimental import pallas as pl
from jax.experimental.pallas import tpu as pltpu
from jax.sharding import PartitionSpec as P

NY, NK, NZ, NX = 8, 2, 8, 4
CHUNK = 4096
LANES = 128
ROWS = 9
PAIR = "pair"


def hops(offset):
    dy, dk, dz, dx = offset
    dx = 1 if dx == PAIR else min(dx, NX - dx)
    return min(dy, NY - dy) + min(dz, NZ - dz) + dx


def far_first(offsets):
    return sorted((o for o in offsets if o != (0, 0, 0, 0)), key=lambda o: -hops(o))


TWIN = (0, 1, 0, 0)
FIRST = far_first(itertools.product(range(NY), (0,), (0,), (0, PAIR)))
SECOND = far_first(itertools.product((0,), (0,), range(NZ), range(NX)))
ALONG_Z = far_first(itertools.product((0,), (0,), range(NZ), (0,)))
ALONG_X = far_first(itertools.product((0,), (0,), (0,), range(NX)))
GREETED = far_first({o for o in FIRST if o != (0, 0, 0, PAIR)} | set(ALONG_Z) | set(ALONG_X) | {TWIN})


class Places:
    def __init__(self):
        row, col = lax.axis_index("row"), lax.axis_index("col")
        self.y, self.k = lax.div(row, 2), lax.rem(row, 2)
        self.z, self.x = lax.div(col, NX), lax.rem(col, NX)
        self.pair_bit = lax.rem(self.x, 2)
        self.ys = [self.y] + [lax.rem(self.y + i, NY) for i in range(1, NY)]
        self.zs = [self.z] + [lax.rem(self.z + i, NZ) for i in range(1, NZ)]
        self.xs = {i: lax.rem(self.x + i, NX) for i in range(1, NX)} | {0: self.x, PAIR: self.x + 1 - 2 * self.pair_bit}
        self.row = {(i, 0): self.ys[i] * NK + self.k for i in range(NY)} | {(0, 1): row + 1 - 2 * self.k}
        self.col = {(i, j): self.zs[i] * NX + self.xs[j] for i in range(NZ) for j in range(NX)}
        self.col[0, PAIR] = self.z * NX + self.xs[PAIR]

    def at(self, offset):
        dy, dk, dz, dx = offset
        return {
            "device_id": (self.row[dy, dk], self.col[dz, dx]),
            "device_id_type": pl.DeviceIdType.MESH,
        }


def sign(bit):
    return (1 - 2 * bit).astype(jnp.float32)


def rows_summed(squares, odd):
    for level in range(3):
        half = squares.shape[1] // 2
        low, high = squares[:, :half], squares[:, half:]
        there = odd[level][:, :half]
        step = 2**level
        squares = jnp.where(there, high, low) + pltpu.roll(jnp.where(there, low, high), 8 - step, 0)
    return squares


def row_walsh(values, row_ids):
    for level in range(3):
        step = 2**level
        up, down = pltpu.roll(values, 8 - step, 0), pltpu.roll(values, step, 0)
        values = jnp.where((row_ids >> level) & 1 == 1, down - values, values + up)
    return values


def walsh_matrix():
    common = lax.broadcasted_iota(jnp.int32, (LANES, LANES), 0) & lax.broadcasted_iota(jnp.int32, (LANES, LANES), 1)
    parity = common ^ (common >> 4)
    parity = parity ^ (parity >> 2)
    parity = (parity ^ (parity >> 1)) & 1
    return (1 - 2 * parity).astype(jnp.float32).astype(jnp.bfloat16)


def walsh_over_first(values):
    count, *rest = values.shape
    for step in (4, 2, 1):
        pairs = values.reshape(count // (2 * step), 2, step, *rest)
        low, high = pairs[:, 0], pairs[:, 1]
        values = jnp.stack([low + high, low - high], axis=1).reshape(count, *rest)
    return values


def wait_for(slots, count, semaphore):
    pltpu.make_async_copy(slots.at[pl.ds(0, count)], slots.at[pl.ds(0, count)], semaphore).wait()


def exchange(amplitudes, out, held, keep, give, got, send1, recv1, send2, recv2, load_sem, twin_sem, sem1, sem2, seen):
    here = Places()

    loads = []
    for part in range(NY):
        columns = pl.ds(part * CHUNK, CHUNK)
        loads.append(pltpu.make_async_copy(amplitudes.at[:, :, columns], held.at[:, :, columns], load_sem.at[part]))
    for load in loads:
        load.start()
    barrier = pltpu.get_barrier_semaphore()
    for offset in GREETED:
        pl.semaphore_signal(barrier, inc=1, **here.at(offset))

    row_ids = lax.broadcasted_iota(jnp.int32, (8, CHUNK // 4), 0)
    odd = [(row_ids >> level) & 1 == 1 for level in range(3)]
    core_sign = sign(here.k)
    mass = jnp.zeros((8, 2 * LANES), jnp.float32)
    for part in range(NY):
        loads[part].wait()
        real = held[0, :, part * CHUNK : (part + 1) * CHUNK]
        imag = held[1, :, part * CHUNK : (part + 1) * CHUNK]
        squares = real * real + imag * imag
        zero, one = rows_summed(squares[:, : CHUNK // 2], odd), rows_summed(squares[:, CHUNK // 2 :], odd)
        mass = mass + (zero + one)
        one = core_sign * one
        keep[part] = zero + one
        give[part] = zero - one
    give[NY] = mass

    pl.semaphore_wait(barrier, len(GREETED))
    for offset in ALONG_Z:
        pl.semaphore_signal(seen, inc=1, **here.at(offset))

    twin = pltpu.make_async_remote_copy(give, got, twin_sem.at[0], twin_sem.at[1], **here.at(TWIN))
    twin.start()
    twin.wait_recv()

    parts = walsh_over_first(keep[...] + got[0:NY])
    mass = mass + got[NY]
    mass = jnp.sum(mass[:, :LANES] + mass[:, LANES:], axis=0, keepdims=True)
    for half in range(2):
        send1[:, half, 0:8, :] = parts[:, :, half * LANES : (half + 1) * LANES]
    send1[:, :, 8:9, :] = jnp.broadcast_to(mass, (NY, 2, 1, LANES))
    slot = here.y * 2 + here.pair_bit
    for offset in FIRST:
        bit = 1 - here.pair_bit if offset[3] == PAIR else here.pair_bit
        pltpu.make_async_remote_copy(
            send1.at[here.ys[offset[0]], bit], recv1.at[slot], sem1.at[0], sem1.at[1], **here.at(offset)
        ).start()
    recv1[slot] = send1[here.y, here.pair_bit]
    wait_for(recv1, len(FIRST), sem1.at[1])

    sums = recv1[...].reshape(NY, 2, ROWS, LANES).sum(axis=0)
    total = sums[0] + sums[1]
    send2[0] = total
    send2[1, 0:8, :] = sums[0, 0:8] - sums[1, 0:8]
    send2[1, 8:9, :] = total[8:9]

    pl.semaphore_wait(seen, len(ALONG_Z))
    slot = here.z * NX + here.x
    bits = {dx: lax.rem(here.xs[dx], 2) for dx in range(NX)}
    for offset in SECOND:
        pltpu.make_async_remote_copy(
            send2.at[bits[offset[3]]], recv2.at[slot], sem2.at[0], sem2.at[1], **here.at(offset)
        ).start()
    recv2[slot] = send2[here.pair_bit]
    matrix = walsh_matrix()
    signs = [sign(lax.rem(lax.div(here.z, 2**level), 2)) for level in (2, 1, 0)] + [sign(lax.div(here.x, 2))]
    wait_for(recv2, len(SECOND), sem2.at[1])

    terms = recv2[...]
    masses = jnp.sum(terms[:, 8:9, :], axis=0)
    terms = terms[:, 0:8, :]
    for factor in signs:
        half = terms.shape[0] // 2
        terms = terms[:half] + factor * terms[half:]
    rows = row_ids[:, :LANES]
    values = jnp.concatenate(
        [
            row_walsh(terms[0] + terms[1], rows),
            row_walsh(terms[0] - terms[1], rows),
            jnp.broadcast_to(masses, (16, LANES)),
        ],
        axis=0,
    )
    high = values.astype(jnp.bfloat16)
    rest = values - high.astype(jnp.float32)
    middle = rest.astype(jnp.bfloat16)
    low = (rest - middle.astype(jnp.float32)).astype(jnp.bfloat16)
    product = jnp.dot(jnp.concatenate([high, middle, low], axis=0), matrix, preferred_element_type=jnp.float32)
    out[...] = product[0:24] + product[32:56] + product[64:88]
    twin.wait_send()
    wait_for(recv1, len(FIRST), sem1.at[0])
    wait_for(recv2, len(SECOND), sem2.at[0])


def reorder(order, values, out):
    target = lax.broadcasted_iota(jnp.int32, (16, LANES), 0) * LANES + lax.broadcasted_iota(jnp.int32, (16, LANES), 1)
    source = jnp.zeros_like(target)
    for location in range(11):
        source = source + (((target >> location) & 1) << order[location])
    lane, row = source & 127, source >> 7
    row = ((row & 1) << 3) | ((row >> 3) & 1) | ((row >> 1) & 2) | ((row << 1) & 4)
    result = jnp.zeros((16, LANES), jnp.float32)
    for i in range(16):
        line = jnp.broadcast_to(values[i : i + 1, :], (16, LANES))
        result = jnp.where(row == i, jnp.take_along_axis(line, lane, axis=1), result)
    total = jnp.broadcast_to(values[16:17, 0:1], (16, LANES))
    out[...] = result * 2048.0 / total


def local(amplitudes, qubit_order):
    vmem = pl.BlockSpec(memory_space=pltpu.VMEM)
    f32 = jnp.float32
    values = pl.pallas_call(
        exchange,
        out_shape=jax.ShapeDtypeStruct((24, LANES), f32),
        in_specs=[pl.BlockSpec(memory_space=pl.ANY)],
        out_specs=vmem,
        scratch_shapes=[
            pltpu.VMEM((2, 8, NY * CHUNK), f32),
            pltpu.VMEM((NY, 8, 2 * LANES), f32),
            pltpu.VMEM((NY + 1, 8, 2 * LANES), f32),
            pltpu.VMEM((NY + 1, 8, 2 * LANES), f32),
            pltpu.VMEM((NY, 2, ROWS, LANES), f32),
            pltpu.VMEM((2 * NY, ROWS, LANES), f32),
            pltpu.VMEM((2, ROWS, LANES), f32),
            pltpu.VMEM((NZ * NX, ROWS, LANES), f32),
            pltpu.SemaphoreType.DMA((NY,)),
            pltpu.SemaphoreType.DMA((2,)),
            pltpu.SemaphoreType.DMA((2,)),
            pltpu.SemaphoreType.DMA((2,)),
            pltpu.SemaphoreType.REGULAR,
        ],
        compiler_params=pltpu.CompilerParams(
            collective_id=0, has_side_effects=True, vmem_limit_bytes=56 * 2**20
        ),
    )(amplitudes)
    result = pl.pallas_call(
        reorder,
        out_shape=jax.ShapeDtypeStruct((16, LANES), f32),
        in_specs=[pl.BlockSpec(memory_space=pltpu.SMEM), vmem],
        out_specs=vmem,
    )(qubit_order, values)
    return result.reshape(1, -1)


def solution(mesh):
    return jax.shard_map(
        local, mesh=mesh, in_specs=(P(None, "row", "col"), P()), out_specs=P("col", "row"), check_vma=False
    )
```

time: 116 us -> 29.6 us (0.26)
  the two profiles are of different devices: /device:TPU:2 before, /device:TPU:1 now
where the time goes in v1:
time: 29.6 us; the launch traced here: 29.4 us
  Pallas kernels  29.4 us (99%)
    pallas_call x1, Pallas kernels, local(): pl.pallas_call(exchange, out_shape=jax.ShapeDtypeStruct((24, LANES), f32)...  28 us
    pallas_call x1, Pallas kernels, local(): pl.pallas_call(reorder, out_shape=jax.ShapeDtypeStruct((16, LANES), f32),...  1.45 us

profile of v1, /device:TPU:1, one launch (start us, length us, event | category | flops | bytes accessed | tf_op | source)
XLA Modules:
  0.0 29.4 jit_solution(4977523382771044913)
XLA Ops:
  0.0 28.0 %shard_map.28.values = f32[24,128]{1,0:T(8,128)} custom-call(f32[2,8,32768]{2,1,0:T(8,128)} %amplitudes.1), custom_call_target="tpu_custom_call" | custom-call | tf_op jit(solution)/shard_map/pallas_call | solution.py:214
  28.0 1.5 %shard_map.29 = f32[16,128]{1,0:T(8,128)} custom-call(s32[11]{0:T(128)} %order.1, f32[24,128]{1,0:T(8,128)} %shard_map.28.values), custom_call_target="tpu_custom_call" | custom-call | tf_op jit(solution)/shard_map/pallas_call | solution.py:238

commit v2 on v1

--- a/solution.py
+++ b/solution.py
@@ -26,11 +26,16 @@
 
 
 TWIN = (0, 1, 0, 0)
-FIRST = far_first(itertools.product(range(NY), (0,), (0,), (0, PAIR)))
+FAR_Y = (4,)
+FAR = far_first(itertools.product(FAR_Y, range(NK), (0,), (0, PAIR)))
+NEAR = far_first(o for o in itertools.product(range(NY), (0,), (0,), (0, PAIR)) if o[0] not in FAR_Y)
+SLOTS = sorted(FAR + NEAR, key=lambda o: o[3] == PAIR)
+OWN_SIDE = sum(o[3] != PAIR for o in SLOTS)
 SECOND = far_first(itertools.product((0,), (0,), range(NZ), range(NX)))
-ALONG_Z = far_first(itertools.product((0,), (0,), range(NZ), (0,)))
+NEXT_Z = [(0, 0, 1, 0), (0, 0, NZ - 1, 0)]
+SECOND_Z = [(0, 0, 2, 0), (0, 0, NZ - 2, 0)]
 ALONG_X = far_first(itertools.product((0,), (0,), (0,), range(NX)))
-GREETED = far_first({o for o in FIRST if o != (0, 0, 0, PAIR)} | set(ALONG_Z) | set(ALONG_X) | {TWIN})
+GREETED = far_first({o for o in FAR + NEAR if o != (0, 0, 0, PAIR)} | set(NEXT_Z) | set(ALONG_X) | {TWIN})
 
 
 class Places:
@@ -42,7 +47,8 @@
         self.ys = [self.y] + [lax.rem(self.y + i, NY) for i in range(1, NY)]
         self.zs = [self.z] + [lax.rem(self.z + i, NZ) for i in range(1, NZ)]
         self.xs = {i: lax.rem(self.x + i, NX) for i in range(1, NX)} | {0: self.x, PAIR: self.x + 1 - 2 * self.pair_bit}
-        self.row = {(i, 0): self.ys[i] * NK + self.k for i in range(NY)} | {(0, 1): row + 1 - 2 * self.k}
+        other = 1 - self.k
+        self.row = {(i, j): self.ys[i] * NK + (other if j else self.k) for i in range(NY) for j in range(NK)}
         self.col = {(i, j): self.zs[i] * NX + self.xs[j] for i in range(NZ) for j in range(NX)}
         self.col[0, PAIR] = self.z * NX + self.xs[PAIR]
 
@@ -97,7 +103,10 @@
     pltpu.make_async_copy(slots.at[pl.ds(0, count)], slots.at[pl.ds(0, count)], semaphore).wait()
 
 
-def exchange(amplitudes, out, held, keep, give, got, send1, recv1, send2, recv2, load_sem, twin_sem, sem1, sem2, seen):
+def exchange(
+    amplitudes, qubit_order, out, lanes, lines,
+    held, order, keep, give, got, own, sent, recv1, send2, recv2, load_sem, order_sem, twin_sem, far_sem, near_sem, sem2, seen,
+):
     here = Places()
 
     loads = []
@@ -106,6 +115,8 @@
         loads.append(pltpu.make_async_copy(amplitudes.at[:, :, columns], held.at[:, :, columns], load_sem.at[part]))
     for load in loads:
         load.start()
+    order_load = pltpu.make_async_copy(qubit_order, order, order_sem)
+    order_load.start()
     barrier = pltpu.get_barrier_semaphore()
     for offset in GREETED:
         pl.semaphore_signal(barrier, inc=1, **here.at(offset))
@@ -124,52 +135,77 @@
         one = core_sign * one
         keep[part] = zero + one
         give[part] = zero - one
+    own_part, other_part = walsh_over_first(keep[...]), walsh_over_first(give[0:NY])
+    give[0:NY] = other_part
     give[NY] = mass
+    own_mass = jnp.sum(mass[:, :LANES] + mass[:, LANES:], axis=0, keepdims=True)
+    spread = jnp.broadcast_to(own_mass, (NY, 1, LANES))
+    for which, part in enumerate((own_part, other_part)):
+        for half in range(2):
+            own[which, half, :, 0:8, :] = part[:, :, half * LANES : (half + 1) * LANES]
+            own[which, half, :, 8:9, :] = spread
 
     pl.semaphore_wait(barrier, len(GREETED))
-    for offset in ALONG_Z:
-        pl.semaphore_signal(seen, inc=1, **here.at(offset))
-
     twin = pltpu.make_async_remote_copy(give, got, twin_sem.at[0], twin_sem.at[1], **here.at(TWIN))
     twin.start()
+    sides = {0: here.pair_bit, PAIR: 1 - here.pair_bit}
+    for offset in FAR:
+        pltpu.make_async_remote_copy(
+            own.at[offset[1], sides[offset[3]], here.ys[offset[0]]],
+            recv1.at[SLOTS.index(offset)], far_sem.at[0], far_sem.at[1], **here.at(offset)
+        ).start()
+    for offset in NEXT_Z:
+        pl.semaphore_signal(seen.at[0], inc=1, **here.at(offset))
     twin.wait_recv()
 
-    parts = walsh_over_first(keep[...] + got[0:NY])
-    mass = mass + got[NY]
-    mass = jnp.sum(mass[:, :LANES] + mass[:, LANES:], axis=0, keepdims=True)
+    mass = own_mass + jnp.sum(got[NY, :, :LANES] + got[NY, :, LANES:], axis=0, keepdims=True)
+    spread = jnp.broadcast_to(mass, (NY, 1, LANES))
     for half in range(2):
-        send1[:, half, 0:8, :] = parts[:, :, half * LANES : (half + 1) * LANES]
-    send1[:, :, 8:9, :] = jnp.broadcast_to(mass, (NY, 2, 1, LANES))
-    slot = here.y * 2 + here.pair_bit
-    for offset in FIRST:
-        bit = 1 - here.pair_bit if offset[3] == PAIR else here.pair_bit
+        columns = slice(half * LANES, (half + 1) * LANES)
+        sent[half, :, 0:8, :] = own[0, half, :, 0:8, :] + got[0:NY, :, columns]
+        sent[half, :, 8:9, :] = spread
+    for offset in NEAR:
         pltpu.make_async_remote_copy(
-            send1.at[here.ys[offset[0]], bit], recv1.at[slot], sem1.at[0], sem1.at[1], **here.at(offset)
+            sent.at[sides[offset[3]], here.ys[offset[0]]],
+            recv1.at[SLOTS.index(offset)], near_sem.at[0], near_sem.at[1], **here.at(offset)
         ).start()
-    recv1[slot] = send1[here.y, here.pair_bit]
-    wait_for(recv1, len(FIRST), sem1.at[1])
-
-    sums = recv1[...].reshape(NY, 2, ROWS, LANES).sum(axis=0)
-    total = sums[0] + sums[1]
-    send2[0] = total
-    send2[1, 0:8, :] = sums[0, 0:8] - sums[1, 0:8]
-    send2[1, 8:9, :] = total[8:9]
-
-    pl.semaphore_wait(seen, len(ALONG_Z))
+
+    pl.semaphore_wait(seen.at[0], len(NEXT_Z))
+    for offset in SECOND_Z:
+        pl.semaphore_signal(seen.at[1], inc=1, **here.at(offset))
+    order_load.wait()
+    lanes[...], lines[...] = sources(order)
+    matrix = walsh_matrix()
+    signs = [sign(lax.rem(lax.div(here.z, 2**level), 2)) for level in (2, 1, 0)] + [sign(lax.div(here.x, 2))]
+    pair_sign = sign(here.pair_bit)
+    pl.semaphore_wait(seen.at[1], len(SECOND_Z))
+    for offset in ALONG_X:
+        pl.semaphore_signal(seen.at[2], inc=1, **here.at(offset))
+    pl.semaphore_wait(seen.at[2], len(ALONG_X))
+    wait_for(recv1, len(FAR), far_sem.at[1])
+    wait_for(recv1, len(NEAR), near_sem.at[1])
+
+    this_side = recv1[0:OWN_SIDE].sum(axis=0) + sent[here.pair_bit, here.y]
+    that_side = recv1[OWN_SIDE:].sum(axis=0)
+    send2[0] = this_side + that_side
+    send2[1, 0:8, :] = pair_sign * (this_side[0:8] - that_side[0:8])
+    send2[1, 8:9, :] = this_side[8:9] + that_side[8:9]
+
     slot = here.z * NX + here.x
     bits = {dx: lax.rem(here.xs[dx], 2) for dx in range(NX)}
     for offset in SECOND:
+        with_mass = offset[3] % 2 == 0
+        height, pair = (pl.ds(0, ROWS), 0) if with_mass else (pl.ds(0, 8), 2)
         pltpu.make_async_remote_copy(
-            send2.at[bits[offset[3]]], recv2.at[slot], sem2.at[0], sem2.at[1], **here.at(offset)
+            send2.at[bits[offset[3]], height], recv2.at[slot, height], sem2.at[pair], sem2.at[pair + 1], **here.at(offset)
         ).start()
     recv2[slot] = send2[here.pair_bit]
-    matrix = walsh_matrix()
-    signs = [sign(lax.rem(lax.div(here.z, 2**level), 2)) for level in (2, 1, 0)] + [sign(lax.div(here.x, 2))]
-    wait_for(recv2, len(SECOND), sem2.at[1])
-
-    terms = recv2[...]
-    masses = jnp.sum(terms[:, 8:9, :], axis=0)
-    terms = terms[:, 0:8, :]
+    light = recv2.at[pl.ds(0, NZ * NX // 2), pl.ds(0, 8)]
+    wait_for(recv2, NZ * NX // 2 - 1, sem2.at[1])
+    pltpu.make_async_copy(light, light, sem2.at[3]).wait()
+
+    masses = functools.reduce(jnp.add, [recv2[2 * i + here.pair_bit, 8:9, :] for i in range(NZ * NX // 2)])
+    terms = recv2[:, 0:8, :]
     for factor in signs:
         half = terms.shape[0] // 2
         terms = terms[:half] + factor * terms[half:]
@@ -189,58 +225,68 @@
     product = jnp.dot(jnp.concatenate([high, middle, low], axis=0), matrix, preferred_element_type=jnp.float32)
     out[...] = product[0:24] + product[32:56] + product[64:88]
     twin.wait_send()
-    wait_for(recv1, len(FIRST), sem1.at[0])
-    wait_for(recv2, len(SECOND), sem2.at[0])
-
-
-def reorder(order, values, out):
+    wait_for(recv1, len(FAR), far_sem.at[0])
+    wait_for(recv1, len(NEAR), near_sem.at[0])
+    wait_for(recv2, NZ * NX // 2 - 1, sem2.at[0])
+    pltpu.make_async_copy(light, light, sem2.at[2]).wait()
+
+
+def sources(order):
     target = lax.broadcasted_iota(jnp.int32, (16, LANES), 0) * LANES + lax.broadcasted_iota(jnp.int32, (16, LANES), 1)
     source = jnp.zeros_like(target)
     for location in range(11):
         source = source + (((target >> location) & 1) << order[location])
-    lane, row = source & 127, source >> 7
-    row = ((row & 1) << 3) | ((row >> 3) & 1) | ((row >> 1) & 2) | ((row << 1) & 4)
+    row = source >> 7
+    return source & 127, ((row & 1) << 3) | ((row >> 3) & 1) | ((row >> 1) & 2) | ((row << 1) & 4)
+
+
+def reorder(values, lanes, lines, out):
+    lane, line = lanes[...], lines[...]
     result = jnp.zeros((16, LANES), jnp.float32)
     for i in range(16):
-        line = jnp.broadcast_to(values[i : i + 1, :], (16, LANES))
-        result = jnp.where(row == i, jnp.take_along_axis(line, lane, axis=1), result)
+        row = jnp.broadcast_to(values[i : i + 1, :], (16, LANES))
+        result = jnp.where(line == i, jnp.take_along_axis(row, lane, axis=1), result)
     total = jnp.broadcast_to(values[16:17, 0:1], (16, LANES))
-    out[...] = result * 2048.0 / total
+    out[...] = result * 1024.0 / total
 
 
 def local(amplitudes, qubit_order):
     vmem = pl.BlockSpec(memory_space=pltpu.VMEM)
     f32 = jnp.float32
-    values = pl.pallas_call(
+    tables = pl.pallas_call(
         exchange,
-        out_shape=jax.ShapeDtypeStruct((24, LANES), f32),
-        in_specs=[pl.BlockSpec(memory_space=pl.ANY)],
-        out_specs=vmem,
+        out_shape=[pltpu.VMEM((24, LANES), f32), pltpu.VMEM((16, LANES), jnp.int32), pltpu.VMEM((16, LANES), jnp.int32)],
+        in_specs=[pl.BlockSpec(memory_space=pl.ANY), pl.BlockSpec(memory_space=pl.ANY)],
+        out_specs=[vmem] * 3,
         scratch_shapes=[
             pltpu.VMEM((2, 8, NY * CHUNK), f32),
+            pltpu.SMEM((11,), jnp.int32),
             pltpu.VMEM((NY, 8, 2 * LANES), f32),
             pltpu.VMEM((NY + 1, 8, 2 * LANES), f32),
             pltpu.VMEM((NY + 1, 8, 2 * LANES), f32),
-            pltpu.VMEM((NY, 2, ROWS, LANES), f32),
-            pltpu.VMEM((2 * NY, ROWS, LANES), f32),
+            pltpu.VMEM((NK, 2, NY, ROWS, LANES), f32),
+            pltpu.VMEM((2, NY, ROWS, LANES), f32),
+            pltpu.VMEM((len(SLOTS), ROWS, LANES), f32),
             pltpu.VMEM((2, ROWS, LANES), f32),
             pltpu.VMEM((NZ * NX, ROWS, LANES), f32),
             pltpu.SemaphoreType.DMA((NY,)),
+            pltpu.SemaphoreType.DMA,
             pltpu.SemaphoreType.DMA((2,)),
             pltpu.SemaphoreType.DMA((2,)),
             pltpu.SemaphoreType.DMA((2,)),
-            pltpu.SemaphoreType.REGULAR,
+            pltpu.SemaphoreType.DMA((4,)),
+            pltpu.SemaphoreType.REGULAR((3,)),
         ],
         compiler_params=pltpu.CompilerParams(
             collective_id=0, has_side_effects=True, vmem_limit_bytes=56 * 2**20
         ),
-    )(amplitudes)
+    )(amplitudes, qubit_order)
     result = pl.pallas_call(
         reorder,
         out_shape=jax.ShapeDtypeStruct((16, LANES), f32),
-        in_specs=[pl.BlockSpec(memory_space=pltpu.SMEM), vmem],
+        in_specs=[vmem] * 3,
         out_specs=vmem,
-    )(qubit_order, values)
+    )(*(pltpu.with_memory_space_constraint(table, pltpu.VMEM) for table in tables))
     return result.reshape(1, -1)
 
 

time: 29.6 us -> 27.9 us (0.943)
  Pallas kernels: 29.4 us -> 27.7 us
    pallas_call x1, Pallas kernels: 28 us -> 27 us  [local(): pl.pallas_call(exchange, out_shape=[pltpu.VMEM((24, LANES), f32), pltpu.V...]
    pallas_call x1, Pallas kernels: 1.45 us -> 0.72 us  [local(): pl.pallas_call(reorder, out_shape=jax.ShapeDtypeStruct((16, LANES), f32),...]
where the time goes in v2:
time: 27.9 us; the launch traced here: 27.8 us
  Pallas kernels  27.7 us (99%)
    pallas_call x1, Pallas kernels, local(): pl.pallas_call(exchange, out_shape=[pltpu.VMEM((24, LANES), f32), pltpu.V...  27 us
    pallas_call x1, Pallas kernels, local(): pl.pallas_call(reorder, out_shape=jax.ShapeDtypeStruct((16, LANES), f32),...  0.72 us

profile of v2, /device:TPU:1, one launch (start us, length us, event | category | flops | bytes accessed | tf_op | source)
XLA Modules:
  0.0 27.8 jit_solution(3528057249114519034)
XLA Ops:
  0.0 27.0 %shard_map.28 = (f32[24,128]{1,0:T(8,128)S(1)}, s32[16,128]{1,0:T(8,128)S(1)}, s32[16,128]{1,0:T(8,128)S(1)}) custom-call(f32[2,8,32768]{2,1,0:T(8,128)} %amplitudes.1, s32[11]{0:T(128)} %qubit_order.1), custom_call_target="tpu_custom_call" | custom-call | tf_op jit(solution)/shard_map/pallas_call | solution.py:256
  27.0 0.7 %shard_map.29 = f32[16,128]{1,0:T(8,128)} custom-call(f32[24,128]{1,0:T(8,128)S(1)} %get-tuple-element.8.values, s32[16,128]{1,0:T(8,128)S(1)} %get-tuple-element.9.lanes, s32[16,128]{1,0:T(8,128)S(1)} %get-tuple-element.10.lines), custom_call_target="tpu_custom_call" | custom-call | tf_op jit(solution)/shard_map/pallas_call | solution.py:284

commit v3 on v2

--- a/solution.py
+++ b/solution.py
@@ -31,11 +31,8 @@
 NEAR = far_first(o for o in itertools.product(range(NY), (0,), (0,), (0, PAIR)) if o[0] not in FAR_Y)
 SLOTS = sorted(FAR + NEAR, key=lambda o: o[3] == PAIR)
 OWN_SIDE = sum(o[3] != PAIR for o in SLOTS)
-SECOND = far_first(itertools.product((0,), (0,), range(NZ), range(NX)))
-NEXT_Z = [(0, 0, 1, 0), (0, 0, NZ - 1, 0)]
-SECOND_Z = [(0, 0, 2, 0), (0, 0, NZ - 2, 0)]
 ALONG_X = far_first(itertools.product((0,), (0,), (0,), range(NX)))
-GREETED = far_first({o for o in FAR + NEAR if o != (0, 0, 0, PAIR)} | set(NEXT_Z) | set(ALONG_X) | {TWIN})
+GREETED = far_first({o for o in FAR + NEAR if o != (0, 0, 0, PAIR)} | set(ALONG_X) | {TWIN})
 
 
 class Places:
@@ -52,6 +49,12 @@
         self.col = {(i, j): self.zs[i] * NX + self.xs[j] for i in range(NZ) for j in range(NX)}
         self.col[0, PAIR] = self.z * NX + self.xs[PAIR]
 
+    def at_z(self, z, dx=0):
+        return {
+            "device_id": (self.row[0, 0], z * NX + self.xs[dx]),
+            "device_id_type": pl.DeviceIdType.MESH,
+        }
+
     def at(self, offset):
         dy, dk, dz, dx = offset
         return {
@@ -120,6 +123,10 @@
     barrier = pltpu.get_barrier_semaphore()
     for offset in GREETED:
         pl.semaphore_signal(barrier, inc=1, **here.at(offset))
+    for z in range(NZ - 1, 0, -1):
+        @pl.when(z > here.z)
+        def _():
+            pl.semaphore_signal(barrier, inc=1, **here.at_z(z))
 
     row_ids = lax.broadcasted_iota(jnp.int32, (8, CHUNK // 4), 0)
     odd = [(row_ids >> level) & 1 == 1 for level in range(3)]
@@ -145,7 +152,7 @@
             own[which, half, :, 0:8, :] = part[:, :, half * LANES : (half + 1) * LANES]
             own[which, half, :, 8:9, :] = spread
 
-    pl.semaphore_wait(barrier, len(GREETED))
+    pl.semaphore_wait(barrier, len(GREETED) + here.z)
     twin = pltpu.make_async_remote_copy(give, got, twin_sem.at[0], twin_sem.at[1], **here.at(TWIN))
     twin.start()
     sides = {0: here.pair_bit, PAIR: 1 - here.pair_bit}
@@ -154,8 +161,12 @@
             own.at[offset[1], sides[offset[3]], here.ys[offset[0]]],
             recv1.at[SLOTS.index(offset)], far_sem.at[0], far_sem.at[1], **here.at(offset)
         ).start()
-    for offset in NEXT_Z:
+    for offset in ALONG_X:
         pl.semaphore_signal(seen.at[0], inc=1, **here.at(offset))
+    for z in range(NZ - 1):
+        @pl.when(z < here.z)
+        def _():
+            pl.semaphore_signal(seen.at[1], inc=1, **here.at_z(z))
     twin.wait_recv()
 
     mass = own_mass + jnp.sum(got[NY, :, :LANES] + got[NY, :, LANES:], axis=0, keepdims=True)
@@ -170,18 +181,11 @@
             recv1.at[SLOTS.index(offset)], near_sem.at[0], near_sem.at[1], **here.at(offset)
         ).start()
 
-    pl.semaphore_wait(seen.at[0], len(NEXT_Z))
-    for offset in SECOND_Z:
-        pl.semaphore_signal(seen.at[1], inc=1, **here.at(offset))
     order_load.wait()
     lanes[...], lines[...] = sources(order)
     matrix = walsh_matrix()
     signs = [sign(lax.rem(lax.div(here.z, 2**level), 2)) for level in (2, 1, 0)] + [sign(lax.div(here.x, 2))]
     pair_sign = sign(here.pair_bit)
-    pl.semaphore_wait(seen.at[1], len(SECOND_Z))
-    for offset in ALONG_X:
-        pl.semaphore_signal(seen.at[2], inc=1, **here.at(offset))
-    pl.semaphore_wait(seen.at[2], len(ALONG_X))
     wait_for(recv1, len(FAR), far_sem.at[1])
     wait_for(recv1, len(NEAR), near_sem.at[1])
 
@@ -191,14 +195,23 @@
     send2[1, 0:8, :] = pair_sign * (this_side[0:8] - that_side[0:8])
     send2[1, 8:9, :] = this_side[8:9] + that_side[8:9]
 
+    pl.semaphore_wait(seen.at[0], len(ALONG_X))
     slot = here.z * NX + here.x
     bits = {dx: lax.rem(here.xs[dx], 2) for dx in range(NX)}
-    for offset in SECOND:
-        with_mass = offset[3] % 2 == 0
-        height, pair = (pl.ds(0, ROWS), 0) if with_mass else (pl.ds(0, 8), 2)
-        pltpu.make_async_remote_copy(
-            send2.at[bits[offset[3]], height], recv2.at[slot, height], sem2.at[pair], sem2.at[pair + 1], **here.at(offset)
-        ).start()
+    for z in range(NZ):
+        if z:
+            @pl.when(here.z == z - 1)
+            def _():
+                pl.semaphore_wait(seen.at[1], NZ - z)
+        for dx in (2, 1, 3, 0):
+            height, pair = (pl.ds(0, ROWS), 0) if dx % 2 == 0 else (pl.ds(0, 8), 2)
+            copy = pltpu.make_async_remote_copy(
+                send2.at[bits[dx], height], recv2.at[slot, height], sem2.at[pair], sem2.at[pair + 1], **here.at_z(z, dx)
+            )
+            if dx:
+                copy.start()
+            else:
+                pl.when(here.z != z)(copy.start)
     recv2[slot] = send2[here.pair_bit]
     light = recv2.at[pl.ds(0, NZ * NX // 2), pl.ds(0, 8)]
     wait_for(recv2, NZ * NX // 2 - 1, sem2.at[1])
@@ -275,7 +288,7 @@
             pltpu.SemaphoreType.DMA((2,)),
             pltpu.SemaphoreType.DMA((2,)),
             pltpu.SemaphoreType.DMA((4,)),
-            pltpu.SemaphoreType.REGULAR((3,)),
+            pltpu.SemaphoreType.REGULAR((2,)),
         ],
         compiler_params=pltpu.CompilerParams(
             collective_id=0, has_side_effects=True, vmem_limit_bytes=56 * 2**20

time: 27.9 us -> 26.5 us (0.950)
  Pallas kernels: 27.7 us -> 26.3 us
    pallas_call x1, Pallas kernels: 27 us -> 25.6 us  [local(): pl.pallas_call(exchange, out_shape=[pltpu.VMEM((24, LANES), f32), pltpu.V...]
where the time goes in v3:
time: 26.5 us; the launch traced here: 26.4 us
  Pallas kernels  26.3 us (99%)
    pallas_call x1, Pallas kernels, local(): pl.pallas_call(exchange, out_shape=[pltpu.VMEM((24, LANES), f32), pltpu.V...  25.6 us
    pallas_call x1, Pallas kernels, local(): pl.pallas_call(reorder, out_shape=jax.ShapeDtypeStruct((16, LANES), f32),...  0.72 us

profile of v3, /device:TPU:1, one launch (start us, length us, event | category | flops | bytes accessed | tf_op | source)
XLA Modules:
  0.0 26.4 jit_solution(4332906522658041494)
XLA Ops:
  0.0 25.6 %shard_map.28 = (f32[24,128]{1,0:T(8,128)S(1)}, s32[16,128]{1,0:T(8,128)S(1)}, s32[16,128]{1,0:T(8,128)S(1)}) custom-call(f32[2,8,32768]{2,1,0:T(8,128)} %amplitudes.1, s32[11]{0:T(128)} %qubit_order.1), custom_call_target="tpu_custom_call" | custom-call | tf_op jit(solution)/shard_map/pallas_call | solution.py:269
  25.6 0.7 %shard_map.29 = f32[16,128]{1,0:T(8,128)} custom-call(f32[24,128]{1,0:T(8,128)S(1)} %get-tuple-element.8.values, s32[16,128]{1,0:T(8,128)S(1)} %get-tuple-element.9.lanes, s32[16,128]{1,0:T(8,128)S(1)} %get-tuple-element.10.lines), custom_call_target="tpu_custom_call" | custom-call | tf_op jit(solution)/shard_map/pallas_call | solution.py:297

commit v4 on v3

--- a/solution.py
+++ b/solution.py
@@ -112,6 +112,15 @@
 ):
     here = Places()
 
+    barrier = pltpu.get_barrier_semaphore()
+    for offset in GREETED:
+        pl.semaphore_signal(barrier, inc=1, **here.at(offset))
+    for z in range(NZ - 1, 0, -1):
+        @pl.when(z > here.z)
+        def _():
+            pl.semaphore_signal(barrier, inc=1, **here.at_z(z))
+
+
     loads = []
     for part in range(NY):
         columns = pl.ds(part * CHUNK, CHUNK)
@@ -120,14 +129,6 @@
         load.start()
     order_load = pltpu.make_async_copy(qubit_order, order, order_sem)
     order_load.start()
-    barrier = pltpu.get_barrier_semaphore()
-    for offset in GREETED:
-        pl.semaphore_signal(barrier, inc=1, **here.at(offset))
-    for z in range(NZ - 1, 0, -1):
-        @pl.when(z > here.z)
-        def _():
-            pl.semaphore_signal(barrier, inc=1, **here.at_z(z))
-
     row_ids = lax.broadcasted_iota(jnp.int32, (8, CHUNK // 4), 0)
     odd = [(row_ids >> level) & 1 == 1 for level in range(3)]
     core_sign = sign(here.k)
@@ -144,8 +145,8 @@
         give[part] = zero - one
     own_part, other_part = walsh_over_first(keep[...]), walsh_over_first(give[0:NY])
     give[0:NY] = other_part
-    give[NY] = mass
     own_mass = jnp.sum(mass[:, :LANES] + mass[:, LANES:], axis=0, keepdims=True)
+    give[NY] = jnp.broadcast_to(jnp.concatenate([own_mass, own_mass], axis=1), (8, 2 * LANES))
     spread = jnp.broadcast_to(own_mass, (NY, 1, LANES))
     for which, part in enumerate((own_part, other_part)):
         for half in range(2):
@@ -169,7 +170,7 @@
             pl.semaphore_signal(seen.at[1], inc=1, **here.at_z(z))
     twin.wait_recv()
 
-    mass = own_mass + jnp.sum(got[NY, :, :LANES] + got[NY, :, LANES:], axis=0, keepdims=True)
+    mass = own_mass + got[NY, 0:1, :LANES]
     spread = jnp.broadcast_to(mass, (NY, 1, LANES))
     for half in range(2):
         columns = slice(half * LANES, (half + 1) * LANES)

time: 26.5 us -> 26.5 us (level)
  no operation moved by 1% of the time
where the time goes in v4:
time: 26.5 us; the launch traced here: 26.3 us
  Pallas kernels  26.3 us (99%)
    pallas_call x1, Pallas kernels, local(): pl.pallas_call(exchange, out_shape=[pltpu.VMEM((24, LANES), f32), pltpu.V...  25.6 us
    pallas_call x1, Pallas kernels, local(): pl.pallas_call(reorder, out_shape=jax.ShapeDtypeStruct((16, LANES), f32),...  0.72 us

profile of v4, /device:TPU:1, one launch (start us, length us, event | category | flops | bytes accessed | tf_op | source)
XLA Modules:
  0.0 26.3 jit_solution(11973228451033736886)
XLA Ops:
  0.0 25.6 %shard_map.28 = (f32[24,128]{1,0:T(8,128)S(1)}, s32[16,128]{1,0:T(8,128)S(1)}, s32[16,128]{1,0:T(8,128)S(1)}) custom-call(f32[2,8,32768]{2,1,0:T(8,128)} %amplitudes.1, s32[11]{0:T(128)} %qubit_order.1), custom_call_target="tpu_custom_call" | custom-call | tf_op jit(solution)/shard_map/pallas_call | solution.py:270
  25.6 0.7 %shard_map.29 = f32[16,128]{1,0:T(8,128)} custom-call(f32[24,128]{1,0:T(8,128)S(1)} %get-tuple-element.8.values, s32[16,128]{1,0:T(8,128)S(1)} %get-tuple-element.9.lanes, s32[16,128]{1,0:T(8,128)S(1)} %get-tuple-element.10.lines), custom_call_target="tpu_custom_call" | custom-call | tf_op jit(solution)/shard_map/pallas_call | solution.py:298

commit v5 on v3

--- a/solution.py
+++ b/solution.py
@@ -186,6 +186,9 @@
     matrix = walsh_matrix()
     signs = [sign(lax.rem(lax.div(here.z, 2**level), 2)) for level in (2, 1, 0)] + [sign(lax.div(here.x, 2))]
     pair_sign = sign(here.pair_bit)
+    pl.semaphore_wait(seen.at[0], len(ALONG_X))
+    slot = here.z * NX + here.x
+    bits = {dx: lax.rem(here.xs[dx], 2) for dx in range(NX)}
     wait_for(recv1, len(FAR), far_sem.at[1])
     wait_for(recv1, len(NEAR), near_sem.at[1])
 
@@ -195,9 +198,6 @@
     send2[1, 0:8, :] = pair_sign * (this_side[0:8] - that_side[0:8])
     send2[1, 8:9, :] = this_side[8:9] + that_side[8:9]
 
-    pl.semaphore_wait(seen.at[0], len(ALONG_X))
-    slot = here.z * NX + here.x
-    bits = {dx: lax.rem(here.xs[dx], 2) for dx in range(NX)}
     for z in range(NZ):
         if z:
             @pl.when(here.z == z - 1)

time: 26.5 us -> 26.5 us (level)
  no operation moved by 1% of the time
where the time goes in v5:
time: 26.5 us; the launch traced here: 26.3 us
  Pallas kernels  26.3 us (99%)
    pallas_call x1, Pallas kernels, local(): pl.pallas_call(exchange, out_shape=[pltpu.VMEM((24, LANES), f32), pltpu.V...  25.6 us
    pallas_call x1, Pallas kernels, local(): pl.pallas_call(reorder, out_shape=jax.ShapeDtypeStruct((16, LANES), f32),...  0.72 us

profile of v5, /device:TPU:1, one launch (start us, length us, event | category | flops | bytes accessed | tf_op | source)
XLA Modules:
  0.0 26.3 jit_solution(5394507215355535381)
XLA Ops:
  0.0 25.6 %shard_map.28 = (f32[24,128]{1,0:T(8,128)S(1)}, s32[16,128]{1,0:T(8,128)S(1)}, s32[16,128]{1,0:T(8,128)S(1)}) custom-call(f32[2,8,32768]{2,1,0:T(8,128)} %amplitudes.1, s32[11]{0:T(128)} %qubit_order.1), custom_call_target="tpu_custom_call" | custom-call | tf_op jit(solution)/shard_map/pallas_call | solution.py:269
  25.6 0.7 %shard_map.29 = f32[16,128]{1,0:T(8,128)} custom-call(f32[24,128]{1,0:T(8,128)S(1)} %get-tuple-element.8.values, s32[16,128]{1,0:T(8,128)S(1)} %get-tuple-element.9.lanes, s32[16,128]{1,0:T(8,128)S(1)} %get-tuple-element.10.lines), custom_call_target="tpu_custom_call" | custom-call | tf_op jit(solution)/shard_map/pallas_call | solution.py:297

commit v6 on v5

--- a/solution.py
+++ b/solution.py
@@ -144,8 +144,8 @@
         give[part] = zero - one
     own_part, other_part = walsh_over_first(keep[...]), walsh_over_first(give[0:NY])
     give[0:NY] = other_part
-    give[NY] = mass
     own_mass = jnp.sum(mass[:, :LANES] + mass[:, LANES:], axis=0, keepdims=True)
+    give[NY] = jnp.broadcast_to(jnp.concatenate([own_mass, own_mass], axis=1), (8, 2 * LANES))
     spread = jnp.broadcast_to(own_mass, (NY, 1, LANES))
     for which, part in enumerate((own_part, other_part)):
         for half in range(2):
@@ -169,7 +169,7 @@
             pl.semaphore_signal(seen.at[1], inc=1, **here.at_z(z))
     twin.wait_recv()
 
-    mass = own_mass + jnp.sum(got[NY, :, :LANES] + got[NY, :, LANES:], axis=0, keepdims=True)
+    mass = own_mass + got[NY, 0:1, :LANES]
     spread = jnp.broadcast_to(mass, (NY, 1, LANES))
     for half in range(2):
         columns = slice(half * LANES, (half + 1) * LANES)

time: 26.5 us -> 26.5 us (level)
  no operation moved by 1% of the time
where the time goes in v6:
time: 26.5 us; the launch traced here: 26.3 us
  Pallas kernels  26.3 us (99%)
    pallas_call x1, Pallas kernels, local(): pl.pallas_call(exchange, out_shape=[pltpu.VMEM((24, LANES), f32), pltpu.V...  25.6 us
    pallas_call x1, Pallas kernels, local(): pl.pallas_call(reorder, out_shape=jax.ShapeDtypeStruct((16, LANES), f32),...  0.72 us

profile of v6, /device:TPU:1, one launch (start us, length us, event | category | flops | bytes accessed | tf_op | source)
XLA Modules:
  0.0 26.3 jit_solution(6138039996358709035)
XLA Ops:
  0.0 25.6 %shard_map.28 = (f32[24,128]{1,0:T(8,128)S(1)}, s32[16,128]{1,0:T(8,128)S(1)}, s32[16,128]{1,0:T(8,128)S(1)}) custom-call(f32[2,8,32768]{2,1,0:T(8,128)} %amplitudes.1, s32[11]{0:T(128)} %qubit_order.1), custom_call_target="tpu_custom_call" | custom-call | tf_op jit(solution)/shard_map/pallas_call | solution.py:269
  25.6 0.7 %shard_map.29 = f32[16,128]{1,0:T(8,128)} custom-call(f32[24,128]{1,0:T(8,128)S(1)} %get-tuple-element.8.values, s32[16,128]{1,0:T(8,128)S(1)} %get-tuple-element.9.lanes, s32[16,128]{1,0:T(8,128)S(1)} %get-tuple-element.10.lines), custom_call_target="tpu_custom_call" | custom-call | tf_op jit(solution)/shard_map/pallas_call | solution.py:297
